TPU v7x, 512 devices: a whole 4x4x16 slice. The times are simulated.
512 devices in a mesh: op: 128 (over x_hi, y, z), sec: 4 (over x_lo, core).
Axes of the slice: x: 4 (x_hi: 2, x_lo: 2; x = x_hi * 2 + x_lo), y: 4, z: 16, core: 2. Of those that a mesh axis runs over, the one named last changes fastest.
Arguments:
- wavefunction: float32 [2, 4, 256, 256], P(None, 'sec'), may hold values from -6 to 6
- left_ops: float32 [1024, 4, 256, 256], P('op', 'sec'), may hold values from -0.125 to 0.125
- right_ops: float32 [1024, 4, 256, 256], P('op', 'sec'), may hold values from -0.375 to 0.375
- term_shift: int32 [1024], P('op'), may hold values from -1 to 1
- term_count: int32 [128], P('op'), may hold values from 1 to 8, as said below
- sector_dims: int32 [4], P('sec'), may hold values from 64 to 256, as said below
Outputs:
- sigma: float32 [2, 4, 256, 256], P(None, 'sec', 'op')
Inputs may be any that keep to these rules, and one draw needn't show every extreme that they name: `term_count`: live term slots of an index of op are its first ones; some index has all 8 live. `sector_dims`: some sector has the full dimension 256.
All inputs are finite; a program needn't handle non-finite values.
Results may differ from a plain program's by a relative error of at most 0.0003.
Values sent between devices are 32-bit elements; how exact they have to be, the bound alone decides.
A program may use at most 64 MiB of HBM per device.

v0:
```python
import jax
import jax.numpy as jnp
from jax import lax
from jax.sharding import PartitionSpec as P


def padded(x, sides, width):
    for axis, dim in sides:
        size, length = (lax.axis_size(axis), x.shape[dim])
        up = [(i, (i + 1) % size) for i in range(size - 1)]
        down = [(j, i) for i, j in up]
        last = lax.slice_in_dim(x, length - width, length, axis=dim)
        leading = lax.slice_in_dim(x, 0, width, axis=dim)
        before = lax.ppermute(last, axis, up)
        after = lax.ppermute(leading, axis, down)
        x = jnp.concatenate([before, x, after], axis=dim)
    return x


def shards(wavefunction, left_ops, right_ops, term_shift, term_count, sector_dims):
    local_sectors = wavefunction.shape[1]
    block_dim = wavefunction.shape[2]
    slot_total = left_ops.shape[0]
    row_index = jnp.arange(block_dim, dtype=jnp.int32)
    row_mask = (row_index[None, :] < sector_dims[:, None]).astype(jnp.float32)
    masked = wavefunction * row_mask[None, :, :, None]
    extended = padded(masked, (("sec", 1),), 1)
    live_count = term_count[0]

    def select_blocks(offset):
        return lax.dynamic_slice_in_dim(extended, 1 - offset, local_sectors, 1)

    share_rows = block_dim // lax.axis_size("op")
    first_own = lax.axis_index("op") * share_rows
    live_weight = (jnp.arange(slot_total, dtype=jnp.int32) < live_count).astype(jnp.float32)
    chosen = jax.vmap(select_blocks)(term_shift)
    half = jnp.einsum("kvjab,kjcb->kvjac", chosen, right_ops, precision=lax.Precision.HIGHEST)
    left_rows = left_ops
    left_rows = left_rows * live_weight[:, None, None, None]
    totals = lax.psum(
        jnp.einsum("kjrb,kvjbc->rvjc", left_rows, half, precision=lax.Precision.HIGHEST), "op"
    )
    own_rows = lax.dynamic_slice_in_dim(totals, first_own, share_rows, 0)
    own_mask = lax.dynamic_slice_in_dim(row_mask, first_own, share_rows, 1)
    result = jnp.transpose(own_rows, (1, 2, 0, 3))
    return result * own_mask[None, :, :, None]


def solution(mesh):
    in_specs = (
        P(None, "sec", None, None),
        P("op", "sec", None, None),
        P("op", "sec", None, None),
        P("op"),
        P("op"),
        P("sec"),
    )
    out_specs = P(None, "sec", "op", None)
    return jax.shard_map(shards, mesh=mesh, in_specs=in_specs, out_specs=out_specs, check_vma=False)
```

profile of v0, /device:TPU:6, one launch (start us, length us, event | category | flops | bytes accessed | tf_op | source)
XLA Modules:
  0.0 1322.6 jit_solution(8423953710189432533)
XLA Ops:
  6.5 0.0 copy-start
  6.5 0.0 all-reduce.2.cloned.1.call-start
  7.4 1.1 bitcast_multiply_fusion
  8.5 1.9 collective-permute-start
  10.4 3.6 collective-permute-start.1
  14.7 0.7 fusion.12
  15.4 3.6 collective-permute-done
  19.0 1.8 collective-permute-done.1
  20.8 1.3 pad_maximum_fusion
  22.0 4.2 gather_fusion
  26.2 0.0 copy-done
  26.2 0.0 copy-start.1
  26.2 5.7 fusion
  31.9 0.0 copy-done.1
  32.0 4.3 fusion.6
  36.3 0.0 all-reduce.2.cloned.1.call-update
  36.3 1277.6 %all-reduce.2.cloned.1.call-done = f32[256,2,1,256]{0,3,1,2:T(8,128)} async-done(((f32[256,2,1,256]{0,3,1,2:T(8,128)}), f32[256,2,1,256]{0,3,1,2:T(8,128)}) %all-reduce.2.cloned.1.call-update) | async-done | bytes 524304 | tf_op jit(solution)/shard_map/psum | solution.py:40
  1313.9 1.1 multiply_bitcast_fusion
  1315.0 0.7 copy.8
  (3 shorter events, 0.0 us)
Async XLA Ops:
  6.5 19.7 %copy-start = (f32[8,1,256,256]{3,2,1,0:T(8,128)S(1)}, f32[8,1,256,256]{3,2,1,0:T(8,128)}, u32[]{:S(2)}) copy-start(f32[8,1,256,256]{3,2,1,0:T(8,128)} %param.8) | copy-start | bytes 6291460
  6.5 1307.4 %all-reduce.2.cloned.1.call-start = ((), (), s32[]{:S(2)}) async-start(), calls=%async_computation | async-start | bytes 1048576 | tf_op jit(solution)/shard_map/psum | solution.py:40
  8.5 10.5 collective-permute-start
  10.4 10.3 collective-permute-start.1
  26.2 5.7 copy-start.1
Sparse Core Ops, SparseCore 0:
  36.4 1277.4 all-reduce.1
where the time goes:
time: 1320 us
  waiting for transfers between devices  1280 us (97%)
  between operations  14.9 us (1%)
    psum x1, waiting for transfers between devices, shards(): lax.psum(jnp.einsum('kjrb,kvjbc->rvjc', left_rows, half, precision=lax.Pr...  1280 us
  transfers between devices with their start and end apart: 3, of which 3 were waited for; matrix products, arithmetic and copies ran while one was open for 0% of the time, Pallas kernels for 0%

commit v1 on v0

v1 whole, which is shorter than its diff:
```python
import jax
import jax.numpy as jnp
from jax import lax
from jax.experimental import pallas as pl
from jax.experimental.pallas import tpu as pltpu
from jax.sharding import PartitionSpec as P

MESH = pl.DeviceIdType.MESH
F32, BF16 = jnp.float32, jnp.bfloat16
XH, Y, Z = 2, 4, 16
VECS, B, KT = 2, 256, 8
OWN = B // (XH * Y)
NEAR = [(a, b) for a in range(XH) for b in range(Y) if (a, b) != (0, 0)]
NN = (((1,), (0,)), ((), ()))
NT = (((1,), (1,)), ((), ()))


def split(x):
    hi = x.astype(BF16)
    return hi, (x - hi.astype(F32)).astype(BF16)


def dot3(ah, al, bh, bl, dims):
    def dot(a, b):
        return lax.dot_general(a, b, dims, preferred_element_type=F32)

    return dot(ah, bh) + dot(ah, bl) + dot(al, bh)


def kernel(
    shift_ref, count_ref, dims_ref, w_hbm, l_hbm, r_hbm, out_ref,
    wv, lv, rv, got, sh, sl, lh, ll, rh, rl, gh, gl, part, near_buf, zsrc, zbuf,
    load_sem, ex_send, ex_recv, near_send, near_recv, z_send, z_recv,
):
    op, sec = lax.axis_index("op"), lax.axis_index("sec")
    xh, y, z = op // (Y * Z), (op // Z) % Y, op % Z

    def place(a, b, c):
        return (a * (Y * Z) + b * Z + c, sec)

    load_w = pltpu.make_async_copy(w_hbm, wv, load_sem.at[0])
    load_l = pltpu.make_async_copy(l_hbm, lv, load_sem.at[1])
    load_r = pltpu.make_async_copy(r_hbm, rv, load_sem.at[2])
    load_w.start()
    load_l.start()
    load_r.start()

    barrier = pltpu.get_barrier_semaphore()
    other_op = (1 - xh) * (Y * Z) + y * Z + z

    def greet(target):
        pl.semaphore_signal(barrier, inc=1, device_id=target, device_id_type=MESH)

    for a, b in NEAR:
        greet(place((xh + a) % XH, (y + b) % Y, z))
    for c in range(1, Z):
        greet(place(xh, y, (z + c) % Z))
    up = jnp.where(sec < 3, sec + 1, sec - 3)
    down = jnp.where(sec > 0, sec - 1, sec + 3)
    for a in (op, other_op):
        greet((a, up))
        greet((a, down))

    load_w.wait()
    rows = dims_ref[0]
    row = lax.broadcasted_iota(jnp.int32, (B, B), 0)
    for v in range(VECS):
        m = jnp.where(row < rows, wv[v], 0.0)
        wv[v] = m
        h, l = split(m)
        sh[1, :, v * B : (v + 1) * B] = h
        sl[1, :, v * B : (v + 1) * B] = l
    sh[3] = jnp.zeros((B, VECS * B), BF16)
    sl[3] = jnp.zeros((B, VECS * B), BF16)

    pl.semaphore_wait(barrier, len(NEAR) + Z - 1 + 4)

    def ways(step):
        cross = (sec == 1) if step == 0 else (sec == 2)
        target = sec + 1 if step == 0 else sec - 1
        second = jnp.where(cross, other_op, op)
        slot = 0 if step == 0 else 1
        copies = []
        for half in range(2):
            for v in range(VECS):
                part_rows = pl.ds(half * (B // 2), B // 2)
                copies.append(
                    pltpu.make_async_remote_copy(
                        src_ref=wv.at[v, part_rows],
                        dst_ref=got.at[slot, v, part_rows],
                        send_sem=ex_send.at[slot, half, v],
                        recv_sem=ex_recv.at[slot, half, v],
                        device_id=(op if half == 0 else second, target),
                        device_id_type=MESH,
                    )
                )
        return copies

    to_next, to_prev = ways(0), ways(1)

    @pl.when(sec < 3)
    def _():
        for c in to_next:
            c.start()

    @pl.when(sec > 0)
    def _():
        for c in to_prev:
            c.start()

    load_l.wait()

    def split_l(t, carry):
        h, l = split(lv[t])
        lh[t] = h
        ll[t] = l
        return carry

    lax.fori_loop(0, KT, split_l, 0)
    load_r.wait()
    for t in range(KT):
        h, l = split(rv[t])
        rh[:, t * B : (t + 1) * B] = h
        rl[:, t * B : (t + 1) * B] = l

    def take(slot, index):
        for v in range(VECS):
            h, l = split(got[slot, v])
            sh[index, :, v * B : (v + 1) * B] = h
            sl[index, :, v * B : (v + 1) * B] = l

    @pl.when(sec > 0)
    def _():
        for c in to_next:
            c.wait_recv()
        take(0, 0)

    @pl.when(sec < 3)
    def _():
        for c in to_prev:
            c.wait_recv()
        take(1, 2)

    half_rows = B // XH
    for t in range(KT):
        s = shift_ref[t]
        at = sec - s
        ok = (t < count_ref[0]) & (at >= 0) & (at <= 3)
        i = jnp.where(ok, 1 - s, 3)
        g = dot3(lh[t], ll[t], sh[i], sl[i], NN)
        h, l = split(g)
        for a in range(XH):
            for v in range(VECS):
                gh[a, v, :, t * B : (t + 1) * B] = h[a * half_rows : (a + 1) * half_rows, v * B : (v + 1) * B]
                gl[a, v, :, t * B : (t + 1) * B] = l[a * half_rows : (a + 1) * half_rows, v * B : (v + 1) * B]

    def near_copy(a, b):
        i = NEAR.index((a, b))
        return pltpu.make_async_remote_copy(
            src_ref=part.at[a, (y + b) % Y],
            dst_ref=near_buf.at[i],
            send_sem=near_send.at[i],
            recv_sem=near_recv.at[i],
            device_id=place((xh + a) % XH, (y + b) % Y, z),
            device_id_type=MESH,
        )

    near = {ab: near_copy(*ab) for ab in NEAR}
    for a in (1, 0):
        which = (xh + a) % XH
        m = VECS * half_rows
        p = dot3(
            gh[which].reshape(m, KT * B), gl[which].reshape(m, KT * B), rh[...], rl[...], NT
        ).reshape(VECS, Y, OWN, B)
        for b in range(Y):
            part[a, b] = p[:, b]
        for b in (2, 1, 3, 0):
            if (a, b) in near:
                near[a, b].start()

    for ab in NEAR:
        near[ab].wait_recv()
    total = part[0, y]
    for i in range(len(NEAR)):
        total = total + near_buf[i]
    for v in range(VECS):
        for rb in range(OWN // 8):
            for ch in range(2):
                zsrc[pl.ds(32 * rb + 2 * v + ch, 8, stride=4), :] = total[v, rb * 8 : rb * 8 + 8, ch * 128 : ch * 128 + 128]

    far = []
    for k in range(1, Z):
        to = (z + k) % Z
        far.append(
            pltpu.make_async_remote_copy(
                src_ref=zsrc.at[pl.ds(pl.multiple_of(to * 8, 8), 8)],
                dst_ref=zbuf.at[pl.ds((k - 1) * 8, 8)],
                send_sem=z_send.at[k - 1],
                recv_sem=z_recv.at[k - 1],
                device_id=place(xh, y, to),
                device_id_type=MESH,
            )
        )
    for k in (8, 7, 9, 6, 10, 5, 11, 4, 12, 3, 13, 2, 14, 1, 15):
        far[k - 1].start()
    for c in far:
        c.wait_recv()
    tile = zsrc[pl.ds(pl.multiple_of(z * 8, 8), 8)]
    for k in range(Z - 1):
        tile = tile + zbuf[k * 8 : k * 8 + 8]
    sub = lax.broadcasted_iota(jnp.int32, (8, 128), 0)
    own_row = 2 * op + jnp.where(sub >= 4, 1, 0)
    tile = jnp.where(own_row < rows, tile, 0.0)
    for s in range(2):
        for v in range(VECS):
            for ch in range(2):
                n = 4 * s + 2 * v + ch
                out_ref[v, 0, s : s + 1, ch * 128 : ch * 128 + 128] = tile[n : n + 1]

    @pl.when(sec < 3)
    def _():
        for c in to_next:
            c.wait_send()

    @pl.when(sec > 0)
    def _():
        for c in to_prev:
            c.wait_send()

    for ab in NEAR:
        near[ab].wait_send()
    for c in far:
        c.wait_send()


def shards(wavefunction, left_ops, right_ops, term_shift, term_count, sector_dims):
    vmem, smem, dma = pltpu.VMEM, pltpu.SMEM, pltpu.SemaphoreType.DMA
    n = len(NEAR)
    return pl.pallas_call(
        kernel,
        out_shape=jax.ShapeDtypeStruct((VECS, 1, 2, B), F32),
        in_specs=[pl.BlockSpec(memory_space=smem)] * 3 + [pl.BlockSpec(memory_space=pl.ANY)] * 3,
        out_specs=pl.BlockSpec(memory_space=vmem),
        scratch_shapes=[
            vmem((VECS, B, B), F32),
            vmem((KT, B, B), F32),
            vmem((KT, B, B), F32),
            vmem((2, VECS, B, B), F32),
            vmem((4, B, VECS * B), BF16),
            vmem((4, B, VECS * B), BF16),
            vmem((KT, B, B), BF16),
            vmem((KT, B, B), BF16),
            vmem((B, KT * B), BF16),
            vmem((B, KT * B), BF16),
            vmem((XH, VECS, B // XH, KT * B), BF16),
            vmem((XH, VECS, B // XH, KT * B), BF16),
            vmem((XH, Y, VECS, OWN, B), F32),
            vmem((n, VECS, OWN, B), F32),
            vmem((Z * 8, 128), F32),
            vmem(((Z - 1) * 8, 128), F32),
            dma((3,)),
            dma((2, 2, VECS)),
            dma((2, 2, VECS)),
            dma((n,)),
            dma((n,)),
            dma((Z - 1,)),
            dma((Z - 1,)),
        ],
        compiler_params=pltpu.CompilerParams(
            collective_id=0, has_side_effects=True, vmem_limit_bytes=56 << 20
        ),
        cost_estimate=pl.CostEstimate(flops=3 * 2**30, bytes_accessed=9 << 19, transcendentals=0),
    )(term_shift, term_count, sector_dims,
      wavefunction.reshape(VECS, B, B), left_ops.reshape(KT, B, B), right_ops.reshape(KT, B, B))


def solution(mesh):
    in_specs = (
        P(None, "sec", None, None),
        P("op", "sec", None, None),
        P("op", "sec", None, None),
        P("op"),
        P("op"),
        P("sec"),
    )
    out_specs = P(None, "sec", "op", None)
    return jax.shard_map(shards, mesh=mesh, in_specs=in_specs, out_specs=out_specs, check_vma=False)
```

time: 1320 us -> 43.2 us (0.03)
  the two profiles are of different devices: /device:TPU:6 before, /device:TPU:1 now
where the time goes in v1:
time: 43.2 us; the launch traced here: 43.1 us
  Pallas kernels  40.5 us (94%)
  between operations  1.3 us (3%)
  local copies, waits for them, and re-layouts  1.28 us (3%)
    pallas_call x1, Pallas kernels, shards(): pl.pallas_call(kernel, out_shape=jax.ShapeDtypeStruct((VECS, 1, 2, B), F3...  40.5 us
    unnamed x1, local copies, waits for them, and re-layouts  1.28 us

profile of v1, /device:TPU:1, one launch (start us, length us, event | category | flops | bytes accessed | tf_op | source)
XLA Modules:
  0.0 43.1 jit_solution(14390475453888215804)
XLA Ops:
  1.3 40.5 %shard_map.64 = f32[2,1,2,256]{3,2,1,0:T(2,128)} custom-call(s32[8]{0:T(128)} %shift_ref.1, s32[1]{0:T(128)S(6)} %copy.8.count_ref, s32[1]{0:T(128)S(6)} %copy.9.dims_ref, f32[2,256,256]{2,1,0:T(8,128)} %bitcast.5, f32[8,256,256]{2,1,0:T(8,128)} %bitcast.3, f32[8,256,256]{2,1,0:T(8,128)} %bitcast.4), custom_call_target="tpu_custom_call" | custom-call | flops 3221225472 | bytes 4718592 | tf_op jit(solution)/shard_map/pallas_call | solution.py:239
  41.8 1.3 %copy.10 = f32[2,1,2,256]{3,2,1,0:T(2,128)} copy(f32[2,1,2,256]{3,2,1,0:T(2,128)} %shard_map.64) | data formatting | bytes 8192

commit v2 on v1

v2 whole, which is shorter than its diff:
```python
import jax
import jax.numpy as jnp
from jax import lax
from jax.experimental import pallas as pl
from jax.experimental.pallas import tpu as pltpu
from jax.sharding import PartitionSpec as P

MESH = pl.DeviceIdType.MESH
F32, BF16 = jnp.float32, jnp.bfloat16
XH, Y, Z = 2, 4, 16
VECS, B, KT = 2, 256, 8
PARTS = 2
CUT = B // (XH * Y * PARTS)
NEAR = [(a, b) for a in range(XH) for b in range(Y) if (a, b) != (0, 0)]
NN = (((1,), (0,)), ((), ()))
NT = (((1,), (1,)), ((), ()))


def split(x):
    hi = x.astype(BF16)
    return hi, (x - hi.astype(F32)).astype(BF16)


def dot(a, b, dims):
    return lax.dot_general(a, b, dims, preferred_element_type=F32)


def kernel(
    shift_hbm, count_hbm, dims_hbm, w_hbm, l_hbm, r_hbm, out_ref,
    shift_ref, count_ref, dims_ref, wv, lv, rv, got, sh, sl, ls, rh, rl, gs, part, near_buf, zsrc, zbuf,
    load_sem, ex_send, ex_recv, near_send, near_recv, z_send, z_recv, know,
):
    op, sec = lax.axis_index("op"), lax.axis_index("sec")
    xh, y, z = op // (Y * Z), (op // Z) % Y, op % Z

    def place(a, b, c):
        return (a * (Y * Z) + b * Z + c, sec)

    def signal(sem, target):
        pl.semaphore_signal(sem, inc=1, device_id=target, device_id_type=MESH)

    barrier = pltpu.get_barrier_semaphore()
    other_op = (1 - xh) * (Y * Z) + y * Z + z
    up = jnp.where(sec < 3, sec + 1, sec - 3)
    down = jnp.where(sec > 0, sec - 1, sec + 3)
    for a in (op, other_op):
        signal(barrier, (a, up))
        signal(barrier, (a, down))
    beside = [place(xh, (y + d) % Y, z) for d in (1, 3)] + [place(xh, y, (z + d) % Z) for d in (1, Z - 1)]
    for target in beside:
        signal(barrier, target)

    loads = [
        pltpu.make_async_copy(s, d, load_sem.at[i])
        for i, (s, d) in enumerate(
            ((dims_hbm, dims_ref), (w_hbm, wv), (l_hbm, lv), (r_hbm, rv), (shift_hbm, shift_ref), (count_hbm, count_ref))
        )
    ]
    for c in loads:
        c.start()

    loads[0].wait()
    loads[1].wait()
    rows = dims_ref[0]
    row = lax.broadcasted_iota(jnp.int32, (B, B), 0)
    for v in range(VECS):
        wv[v] = jnp.where(row < rows, wv[v], 0.0)
    pl.semaphore_wait(barrier, 8)

    def ways(step):
        cross = (sec == 1) if step == 0 else (sec == 2)
        target = sec + 1 if step == 0 else sec - 1
        second = jnp.where(cross, other_op, op)
        slot = 0 if step == 0 else 1
        copies = []
        for v in range(VECS):
            for half in range(2):
                part_rows = pl.ds(half * (B // 2), B // 2)
                copies.append(
                    pltpu.make_async_remote_copy(
                        src_ref=wv.at[v, part_rows],
                        dst_ref=got.at[slot, v, part_rows],
                        send_sem=ex_send.at[slot, half, v],
                        recv_sem=ex_recv.at[slot, half, v],
                        device_id=(op if half == 0 else second, target),
                        device_id_type=MESH,
                    )
                )
        return copies

    to_next, to_prev = ways(0), ways(1)

    @pl.when(sec < 3)
    def _():
        for c in to_next:
            c.start()

    @pl.when(sec > 0)
    def _():
        for c in to_prev:
            c.start()

    for target in beside:
        signal(know.at[0], target)

    for v in range(VECS):
        h, l = split(wv[v])
        sh[v, 1] = h
        sl[v, 1] = l
        sh[v, 3] = jnp.zeros((B, B), BF16)
        sl[v, 3] = jnp.zeros((B, B), BF16)

    loads[2].wait()

    def split_l(t, carry):
        h, l = split(lv[t].reshape(XH * Y, PARTS, CUT, B))
        for c in range(PARTS):
            ls[c, t, : B // PARTS] = h[:, c].reshape(B // PARTS, B)
            ls[c, t, B // PARTS :] = l[:, c].reshape(B // PARTS, B)
        return carry

    lax.fori_loop(0, KT, split_l, 0)
    loads[3].wait()
    for t in range(KT):
        h, l = split(rv[t])
        rh[:, t * B : (t + 1) * B] = h
        rl[:, t * B : (t + 1) * B] = l

    pl.semaphore_wait(know.at[0], 4)
    for d in (2, Z - 2):
        signal(know.at[1], place(xh, y, (z + d) % Z))

    loads[4].wait()
    loads[5].wait()
    index = []
    for t in range(KT):
        s = shift_ref[t]
        at = sec - s
        ok = (t < count_ref[0]) & (at >= 0) & (at <= 3)
        index.append(jnp.where(ok, 1 - s, 3))

    m = B // PARTS

    def left(c, v):
        for t in range(KT):
            i = index[t]
            g = dot(ls[c, t], sh[v, i], NN)
            h, l = split(g[:m] + g[m:] + dot(ls[c, t, :m], sl[v, i], NN))
            gs[c, 0, v, :, t * B : (t + 1) * B] = h
            gs[c, 1, v, :, t * B : (t + 1) * B] = l

    for v in range(VECS):
        for copies, edge, slot, i in ((to_next, sec > 0, 0, 0), (to_prev, sec < 3, 1, 2)):

            @pl.when(edge)
            def _():
                for c in copies[2 * v : 2 * v + 2]:
                    c.wait_recv()
                h, l = split(got[slot, v])
                sh[v, i] = h
                sl[v, i] = l

        if v == VECS - 1:
            for d in (1, 2, 3):
                signal(know.at[2], place(xh, (y + d) % Y, z))
            pl.semaphore_wait(know.at[1], 2)
            for d in (4, Z - 4):
                signal(know.at[3], place(xh, y, (z + d) % Z))
        left(0, v)

    def near_copy(c, a, b):
        i = NEAR.index((a, b))
        to = (xh + a) % XH * Y + (y + b) % Y
        return pltpu.make_async_remote_copy(
            src_ref=part.at[c, to],
            dst_ref=near_buf.at[c, i],
            send_sem=near_send.at[c, i],
            recv_sem=near_recv.at[c, i],
            device_id=(to * Z + z, sec),
            device_id_type=MESH,
        )

    def right(c):
        hi = gs[c].reshape(2 * VECS * m, KT * B)
        p = dot(hi, rh[...], NT)
        n = VECS * m
        p = (p[:n] + p[n:] + dot(gs[c, 0].reshape(n, KT * B), rl[...], NT)).reshape(VECS, XH * Y, CUT, B)
        for q in range(XH * Y):
            part[c, q] = p[:, q]

    near = [[near_copy(c, a, b) for a, b in NEAR] for c in range(PARTS)]
    for c in range(PARTS):
        if c > 0:
            for v in range(VECS):
                left(c, v)
        right(c)
        if c == 0:
            pl.semaphore_wait(know.at[2], 3)
        for a, b in ((1, 2), (1, 1), (1, 3), (1, 0), (0, 2), (0, 1), (0, 3)):
            near[c][NEAR.index((a, b))].start()

    per = Z // PARTS

    def far_copy(c, j):
        to = c * per + j
        slot = (to - z + Z) % Z - 1
        slot = jnp.where(slot < 0, 0, slot)
        return pltpu.make_async_remote_copy(
            src_ref=zsrc.at[c, pl.ds(j * 8, 8)],
            dst_ref=zbuf.at[slot],
            send_sem=z_send.at[to],
            recv_sem=z_recv.at[slot],
            device_id=place(xh, y, to),
            device_id_type=MESH,
        )

    for c in range(PARTS):
        for n in near[c]:
            n.wait_recv()
        total = part[c, xh * Y + y]
        for i in range(len(NEAR)):
            total = total + near_buf[c, i]
        for v in range(VECS):
            for rb in range(CUT // 8):
                for ch in range(2):
                    zsrc[c, pl.ds(32 * rb + 2 * v + ch, 8, stride=4), :] = total[
                        v, rb * 8 : rb * 8 + 8, ch * 128 : ch * 128 + 128
                    ]
        if c == 0:
            pl.semaphore_wait(know.at[3], 2)
        for j in range(per):

            @pl.when(c * per + j != z)
            def _():
                far_copy(c, j).start()

    for k in range(Z - 1):
        pltpu.make_async_remote_copy(
            src_ref=zsrc.at[0, pl.ds(0, 8)],
            dst_ref=zbuf.at[k],
            send_sem=z_send.at[0],
            recv_sem=z_recv.at[k],
            device_id=place(xh, y, (z + 1) % Z),
            device_id_type=MESH,
        ).wait_recv()
    tile = zsrc[z // per, pl.ds(pl.multiple_of(z % per * 8, 8), 8)]
    for k in range(Z - 1):
        tile = tile + zbuf[k]
    sub = lax.broadcasted_iota(jnp.int32, (8, 128), 0)
    own_row = 2 * op + jnp.where(sub >= 4, 1, 0)
    tile = jnp.where(own_row < rows, tile, 0.0)
    for s in range(2):
        out_ref[pl.ds(s, 4, stride=2), :] = tile[4 * s : 4 * s + 4]

    @pl.when(sec < 3)
    def _():
        for c in to_next:
            c.wait_send()

    @pl.when(sec > 0)
    def _():
        for c in to_prev:
            c.wait_send()

    for c in range(PARTS):
        for n in near[c]:
            n.wait_send()
        for j in range(per):

            @pl.when(c * per + j != z)
            def _():
                far_copy(c, j).wait_send()


def shards(wavefunction, left_ops, right_ops, term_shift, term_count, sector_dims):
    vmem, smem, dma = pltpu.VMEM, pltpu.SMEM, pltpu.SemaphoreType.DMA
    n = len(NEAR)
    out = pl.pallas_call(
        kernel,
        out_shape=jax.ShapeDtypeStruct((8, 128), F32),
        in_specs=[pl.BlockSpec(memory_space=pltpu.HBM)] * 3 + [pl.BlockSpec(memory_space=pl.ANY)] * 3,
        out_specs=pl.BlockSpec(memory_space=vmem),
        scratch_shapes=[
            smem((KT,), jnp.int32),
            smem((1,), jnp.int32),
            smem((1,), jnp.int32),
            vmem((VECS, B, B), F32),
            vmem((KT, B, B), F32),
            vmem((KT, B, B), F32),
            vmem((2, VECS, B, B), F32),
            vmem((VECS, 4, B, B), BF16),
            vmem((VECS, 4, B, B), BF16),
            vmem((PARTS, KT, 2 * B // PARTS, B), BF16),
            vmem((B, KT * B), BF16),
            vmem((B, KT * B), BF16),
            vmem((PARTS, 2, VECS, B // PARTS, KT * B), BF16),
            vmem((PARTS, XH * Y, VECS, CUT, B), F32),
            vmem((PARTS, n, VECS, CUT, B), F32),
            vmem((PARTS, Z * 8 // PARTS, 128), F32),
            vmem((Z - 1, 8, 128), F32),
            dma((6,)),
            dma((2, 2, VECS)),
            dma((2, 2, VECS)),
            dma((PARTS, n)),
            dma((PARTS, n)),
            dma((Z,)),
            dma((Z - 1,)),
            pltpu.SemaphoreType.REGULAR((4,)),
        ],
        compiler_params=pltpu.CompilerParams(
            collective_id=0, has_side_effects=True, vmem_limit_bytes=56 << 20
        ),
        cost_estimate=pl.CostEstimate(flops=3 * 2**30, bytes_accessed=9 << 19, transcendentals=0),
    )(term_shift, term_count, sector_dims,
      wavefunction.reshape(VECS, B, B), left_ops.reshape(KT, B, B), right_ops.reshape(KT, B, B))
    return out.reshape(VECS, 2, 2, 128).transpose(0, 2, 1, 3).reshape(VECS, 1, 2, B)


def solution(mesh):
    in_specs = (
        P(None, "sec", None, None),
        P("op", "sec", None, None),
        P("op", "sec", None, None),
        P("op"),
        P("op"),
        P("sec"),
    )
    out_specs = P(None, "sec", "op", None)
    return jax.shard_map(shards, mesh=mesh, in_specs=in_specs, out_specs=out_specs, check_vma=False)
```

time: 43.2 us -> 36.8 us (0.85)
  Pallas kernels: 40.5 us -> 34.1 us
    pallas_call x1, Pallas kernels: 40.5 us -> 34.1 us  [shards(): pl.pallas_call(kernel, out_shape=jax.ShapeDtypeStruct((8, 128), F32), in_...]
where the time goes in v2:
time: 36.8 us; the launch traced here: 36.7 us
  Pallas kernels  34.1 us (93%)
  between operations  1.3 us (4%)
  local copies, waits for them, and re-layouts  1.28 us (3%)
    pallas_call x1, Pallas kernels, shards(): pl.pallas_call(kernel, out_shape=jax.ShapeDtypeStruct((8, 128), F32), in_...  34.1 us
    unnamed x1, local copies, waits for them, and re-layouts  1.28 us

profile of v2, /device:TPU:1, one launch (start us, length us, event | category | flops | bytes accessed | tf_op | source)
XLA Modules:
  0.0 36.7 jit_solution(16806126870863077992)
XLA Ops:
  1.3 34.1 %shard_map.64 = f32[8,128]{1,0:T(8,128)} custom-call(s32[8]{0:T(128)} %shift_hbm.1, s32[1]{0:T(128)S(6)} %copy.9.count_hbm, s32[1]{0:T(128)S(6)} %copy.10.dims_hbm, f32[2,256,256]{2,1,0:T(8,128)} %bitcast.11, f32[8,256,256]{2,1,0:T(8,128)} %bitcast.9, f32[8,256,256]{2,1,0:T(8,128)} %bitcast.10), custom_call_target="tpu_custom_call" | custom-call | flops 3221225472 | bytes 4718592 | tf_op jit(solution)/shard_map/pallas_call | solution.py:278
  35.4 1.3 %copy.11 = f32[2,1,2,256]{3,2,1,0:T(2,128)} copy(f32[2,1,2,256]{3,2,1,0:T(2,128)} %bitcast.8) | data formatting | bytes 8192

commit v3 on v2

--- a/solution.py
+++ b/solution.py
@@ -9,11 +9,13 @@
 F32, BF16 = jnp.float32, jnp.bfloat16
 XH, Y, Z = 2, 4, 16
 VECS, B, KT = 2, 256, 8
-PARTS = 2
-CUT = B // (XH * Y * PARTS)
+HUB = 4
+ENDS = (0, 4, 8, 16)
+PARTS = len(ENDS) - 1
+CUT = [2 * (b - a) for a, b in zip(ENDS, ENDS[1:])]
+ROWS = [XH * Y * n for n in CUT]
 NEAR = [(a, b) for a in range(XH) for b in range(Y) if (a, b) != (0, 0)]
 NN = (((1,), (0,)), ((), ()))
-NT = (((1,), (1,)), ((), ()))
 
 
 def split(x):
@@ -39,6 +41,15 @@
     def signal(sem, target):
         pl.semaphore_signal(sem, inc=1, device_id=target, device_id_type=MESH)
 
+    loads = [
+        pltpu.make_async_copy(s, d, load_sem.at[i])
+        for i, (s, d) in enumerate(
+            ((dims_hbm, dims_ref), (w_hbm, wv), (l_hbm, lv), (r_hbm, rv), (shift_hbm, shift_ref), (count_hbm, count_ref))
+        )
+    ]
+    loads[0].start()
+    loads[1].start()
+
     barrier = pltpu.get_barrier_semaphore()
     other_op = (1 - xh) * (Y * Z) + y * Z + z
     up = jnp.where(sec < 3, sec + 1, sec - 3)
@@ -46,18 +57,17 @@
     for a in (op, other_op):
         signal(barrier, (a, up))
         signal(barrier, (a, down))
-    beside = [place(xh, (y + d) % Y, z) for d in (1, 3)] + [place(xh, y, (z + d) % Z) for d in (1, Z - 1)]
+    beside = [place(xh, (y + d) % Y, z) for d in (1, 3)]
     for target in beside:
         signal(barrier, target)
 
-    loads = [
-        pltpu.make_async_copy(s, d, load_sem.at[i])
-        for i, (s, d) in enumerate(
-            ((dims_hbm, dims_ref), (w_hbm, wv), (l_hbm, lv), (r_hbm, rv), (shift_hbm, shift_ref), (count_hbm, count_ref))
-        )
-    ]
-    for c in loads:
-        c.start()
+    @pl.when(z < HUB)
+    def _():
+        for d in range(1, Z):
+
+            @pl.when(z + d < Z)
+            def _():
+                signal(barrier, place(xh, y, (z + d) % Z))
 
     loads[0].wait()
     loads[1].wait()
@@ -65,7 +75,9 @@
     row = lax.broadcasted_iota(jnp.int32, (B, B), 0)
     for v in range(VECS):
         wv[v] = jnp.where(row < rows, wv[v], 0.0)
-    pl.semaphore_wait(barrier, 8)
+    for i in (2, 3, 4, 5):
+        loads[i].start()
+    pl.semaphore_wait(barrier, 6 + jnp.where(z < HUB, z, HUB))
 
     def ways(step):
         cross = (sec == 1) if step == 0 else (sec == 2)
@@ -102,6 +114,15 @@
 
     for target in beside:
         signal(know.at[0], target)
+    for d in range(HUB):
+
+        @pl.when(z >= HUB)
+        def _():
+            signal(know.at[1], place(xh, y, d))
+
+        @pl.when((z < HUB) & (d < z))
+        def _():
+            signal(know.at[2], place(xh, y, d))
 
     for v in range(VECS):
         h, l = split(wv[v])
@@ -113,22 +134,19 @@
     loads[2].wait()
 
     def split_l(t, carry):
-        h, l = split(lv[t].reshape(XH * Y, PARTS, CUT, B))
+        x = lv[t].reshape(XH * Y, 2 * Z, B)
         for c in range(PARTS):
-            ls[c, t, : B // PARTS] = h[:, c].reshape(B // PARTS, B)
-            ls[c, t, B // PARTS :] = l[:, c].reshape(B // PARTS, B)
+            h, l = split(x[:, 2 * ENDS[c] : 2 * ENDS[c + 1]].reshape(ROWS[c], B))
+            ls[c][t, : ROWS[c]] = h
+            ls[c][t, ROWS[c] :] = l
         return carry
 
     lax.fori_loop(0, KT, split_l, 0)
     loads[3].wait()
     for t in range(KT):
-        h, l = split(rv[t])
-        rh[:, t * B : (t + 1) * B] = h
-        rl[:, t * B : (t + 1) * B] = l
-
-    pl.semaphore_wait(know.at[0], 4)
-    for d in (2, Z - 2):
-        signal(know.at[1], place(xh, y, (z + d) % Z))
+        h, l = split(rv[t].T)
+        rh[t] = h
+        rl[t] = l
 
     loads[4].wait()
     loads[5].wait()
@@ -139,15 +157,27 @@
         ok = (t < count_ref[0]) & (at >= 0) & (at <= 3)
         index.append(jnp.where(ok, 1 - s, 3))
 
-    m = B // PARTS
+    def slab(c, v, i):
+        return (v, i) if c == 0 else (i, v)
 
     def left(c, v):
+        m = ROWS[c]
         for t in range(KT):
             i = index[t]
-            g = dot(ls[c, t], sh[v, i], NN)
-            h, l = split(g[:m] + g[m:] + dot(ls[c, t, :m], sl[v, i], NN))
-            gs[c, 0, v, :, t * B : (t + 1) * B] = h
-            gs[c, 1, v, :, t * B : (t + 1) * B] = l
+            g = dot(ls[c][t], sh[v, i], NN)
+            h, l = split(g[:m] + g[m:] + dot(ls[c][t, :m], sl[v, i], NN))
+            gs[c][(*slab(c, v, 0), slice(None), slice(t * B, (t + 1) * B))] = h
+            gs[c][(*slab(c, v, 1), slice(None), slice(t * B, (t + 1) * B))] = l
+
+    def right(c, vs):
+        n = len(vs) * ROWS[c]
+        both = gs[c][vs[0]] if len(vs) == 1 else gs[c][...]
+        p = dot(both.reshape(2 * n, KT * B), rh[...].reshape(KT * B, B), NN)
+        p = p[:n] + p[n:] + dot(both[0].reshape(n, KT * B), rl[...].reshape(KT * B, B), NN)
+        p = p.reshape(len(vs), XH * Y, CUT[c], B)
+        for k, v in enumerate(vs):
+            for q in range(XH * Y):
+                part[c][q, v] = p[k, q]
 
     for v in range(VECS):
         for copies, edge, slot, i in ((to_next, sec > 0, 0, 0), (to_prev, sec < 3, 1, 2)):
@@ -160,49 +190,38 @@
                 sh[v, i] = h
                 sl[v, i] = l
 
-        if v == VECS - 1:
+        if v == 0:
+            pl.semaphore_wait(know.at[0], 2)
             for d in (1, 2, 3):
-                signal(know.at[2], place(xh, (y + d) % Y, z))
-            pl.semaphore_wait(know.at[1], 2)
-            for d in (4, Z - 4):
-                signal(know.at[3], place(xh, y, (z + d) % Z))
+                signal(know.at[3], place(xh, (y + d) % Y, z))
         left(0, v)
+        right(0, (v,))
 
     def near_copy(c, a, b):
         i = NEAR.index((a, b))
         to = (xh + a) % XH * Y + (y + b) % Y
         return pltpu.make_async_remote_copy(
-            src_ref=part.at[c, to],
-            dst_ref=near_buf.at[c, i],
+            src_ref=part[c].at[to],
+            dst_ref=near_buf[c].at[i],
             send_sem=near_send.at[c, i],
             recv_sem=near_recv.at[c, i],
             device_id=(to * Z + z, sec),
             device_id_type=MESH,
         )
 
-    def right(c):
-        hi = gs[c].reshape(2 * VECS * m, KT * B)
-        p = dot(hi, rh[...], NT)
-        n = VECS * m
-        p = (p[:n] + p[n:] + dot(gs[c, 0].reshape(n, KT * B), rl[...], NT)).reshape(VECS, XH * Y, CUT, B)
-        for q in range(XH * Y):
-            part[c, q] = p[:, q]
-
     near = [[near_copy(c, a, b) for a, b in NEAR] for c in range(PARTS)]
     for c in range(PARTS):
         if c > 0:
             for v in range(VECS):
                 left(c, v)
-        right(c)
+            right(c, (0, 1))
         if c == 0:
-            pl.semaphore_wait(know.at[2], 3)
+            pl.semaphore_wait(know.at[3], 3)
         for a, b in ((1, 2), (1, 1), (1, 3), (1, 0), (0, 2), (0, 1), (0, 3)):
             near[c][NEAR.index((a, b))].start()
 
-    per = Z // PARTS
-
     def far_copy(c, j):
-        to = c * per + j
+        to = ENDS[c] + j
         slot = (to - z + Z) % Z - 1
         slot = jnp.where(slot < 0, 0, slot)
         return pltpu.make_async_remote_copy(
@@ -217,20 +236,36 @@
     for c in range(PARTS):
         for n in near[c]:
             n.wait_recv()
-        total = part[c, xh * Y + y]
+        total = part[c][xh * Y + y]
         for i in range(len(NEAR)):
-            total = total + near_buf[c, i]
+            total = total + near_buf[c][i]
         for v in range(VECS):
-            for rb in range(CUT // 8):
+            for rb in range(CUT[c] // 8):
                 for ch in range(2):
                     zsrc[c, pl.ds(32 * rb + 2 * v + ch, 8, stride=4), :] = total[
                         v, rb * 8 : rb * 8 + 8, ch * 128 : ch * 128 + 128
                     ]
         if c == 0:
-            pl.semaphore_wait(know.at[3], 2)
-        for j in range(per):
-
-            @pl.when(c * per + j != z)
+
+            @pl.when(z < HUB - 1)
+            def _():
+                pl.semaphore_wait(know.at[2], HUB - 1 - z)
+
+        if c == 1:
+
+            @pl.when(z < HUB)
+            def _():
+                pl.semaphore_wait(know.at[1], Z - HUB)
+                for d in range(HUB, Z, HUB):
+                    signal(know.at[4], place(xh, y, z + d))
+
+            @pl.when(z >= HUB)
+            def _():
+                pl.semaphore_wait(know.at[4], 1)
+
+        for j in range(ENDS[c + 1] - ENDS[c]):
+
+            @pl.when(ENDS[c] + j != z)
             def _():
                 far_copy(c, j).start()
 
@@ -243,7 +278,11 @@
             device_id=place(xh, y, (z + 1) % Z),
             device_id_type=MESH,
         ).wait_recv()
-    tile = zsrc[z // per, pl.ds(pl.multiple_of(z % per * 8, 8), 8)]
+    mine, first = 0, 0
+    for c in range(1, PARTS):
+        mine = jnp.where(z >= ENDS[c], c, mine)
+        first = jnp.where(z >= ENDS[c], ENDS[c], first)
+    tile = zsrc[mine, pl.ds(pl.multiple_of((z - first) * 8, 8), 8)]
     for k in range(Z - 1):
         tile = tile + zbuf[k]
     sub = lax.broadcasted_iota(jnp.int32, (8, 128), 0)
@@ -265,9 +304,9 @@
     for c in range(PARTS):
         for n in near[c]:
             n.wait_send()
-        for j in range(per):
-
-            @pl.when(c * per + j != z)
+        for j in range(ENDS[c + 1] - ENDS[c]):
+
+            @pl.when(ENDS[c] + j != z)
             def _():
                 far_copy(c, j).wait_send()
 
@@ -277,7 +316,7 @@
     n = len(NEAR)
     out = pl.pallas_call(
         kernel,
-        out_shape=jax.ShapeDtypeStruct((8, 128), F32),
+        out_shape=vmem((8, 128), F32),
         in_specs=[pl.BlockSpec(memory_space=pltpu.HBM)] * 3 + [pl.BlockSpec(memory_space=pl.ANY)] * 3,
         out_specs=pl.BlockSpec(memory_space=vmem),
         scratch_shapes=[
@@ -290,13 +329,13 @@
             vmem((2, VECS, B, B), F32),
             vmem((VECS, 4, B, B), BF16),
             vmem((VECS, 4, B, B), BF16),
-            vmem((PARTS, KT, 2 * B // PARTS, B), BF16),
-            vmem((B, KT * B), BF16),
-            vmem((B, KT * B), BF16),
-            vmem((PARTS, 2, VECS, B // PARTS, KT * B), BF16),
-            vmem((PARTS, XH * Y, VECS, CUT, B), F32),
-            vmem((PARTS, n, VECS, CUT, B), F32),
-            vmem((PARTS, Z * 8 // PARTS, 128), F32),
+            [vmem((KT, 2 * m, B), BF16) for m in ROWS],
+            vmem((KT, B, B), BF16),
+            vmem((KT, B, B), BF16),
+            [vmem((2, 2, m, KT * B), BF16) for m in ROWS],
+            [vmem((XH * Y, VECS, m, B), F32) for m in CUT],
+            [vmem((n, VECS, m, B), F32) for m in CUT],
+            vmem((PARTS, 4 * max(CUT), 128), F32),
             vmem((Z - 1, 8, 128), F32),
             dma((6,)),
             dma((2, 2, VECS)),
@@ -305,7 +344,7 @@
             dma((PARTS, n)),
             dma((Z,)),
             dma((Z - 1,)),
-            pltpu.SemaphoreType.REGULAR((4,)),
+            pltpu.SemaphoreType.REGULAR((5,)),
         ],
         compiler_params=pltpu.CompilerParams(
             collective_id=0, has_side_effects=True, vmem_limit_bytes=56 << 20

time: 36.8 us -> 34.6 us (0.940)
  Pallas kernels: 34.1 us -> 32.4 us
  local copies, waits for them, and re-layouts: 1.28 us -> 0.6 us
    pallas_call x1, Pallas kernels: 34.1 us -> 32.4 us  [shards(): pl.pallas_call(kernel, out_shape=vmem((8, 128), F32), in_specs=[pl.BlockS...]
    unnamed x1, local copies, waits for them, and re-layouts: 1.28 us -> 0.6 us
where the time goes in v3:
time: 34.6 us; the launch traced here: 34.3 us
  Pallas kernels  32.4 us (94%)
  between operations  1.3 us (4%)
  local copies, waits for them, and re-layouts  0.6 us (2%)
    pallas_call x1, Pallas kernels, shards(): pl.pallas_call(kernel, out_shape=vmem((8, 128), F32), in_specs=[pl.BlockS...  32.4 us

profile of v3, /device:TPU:1, one launch (start us, length us, event | category | flops | bytes accessed | tf_op | source)
XLA Modules:
  0.0 34.3 jit_solution(12475312662616080905)
XLA Ops:
  1.3 32.4 %shard_map.64 = f32[8,128]{1,0:T(8,128)S(1)} custom-call(s32[8]{0:T(128)} %shift_hbm.1, s32[1]{0:T(128)S(6)} %copy.10.count_hbm, s32[1]{0:T(128)S(6)} %copy.11.dims_hbm, f32[2,256,256]{2,1,0:T(8,128)} %bitcast.11, f32[8,256,256]{2,1,0:T(8,128)} %bitcast.9, f32[8,256,256]{2,1,0:T(8,128)} %bitcast.10), custom_call_target="tpu_custom_call" | custom-call | flops 3221225472 | bytes 4718592 | tf_op jit(solution)/shard_map/pallas_call | solution.py:317
  33.7 0.6 %copy.9 = f32[2,1,2,256]{3,2,1,0:T(2,128)} copy(f32[2,1,2,256]{3,2,1,0:T(2,128)S(1)} %bitcast.8) | data formatting | bytes 8192

commit v4 on v3

--- a/solution.py
+++ b/solution.py
@@ -30,7 +30,7 @@
 def kernel(
     shift_hbm, count_hbm, dims_hbm, w_hbm, l_hbm, r_hbm, out_ref,
     shift_ref, count_ref, dims_ref, wv, lv, rv, got, sh, sl, ls, rh, rl, gs, part, near_buf, zsrc, zbuf,
-    load_sem, ex_send, ex_recv, near_send, near_recv, z_send, z_recv, know,
+    load_sem, ex_send, ex_recv, near_send, near_recv, z_sem, know,
 ):
     op, sec = lax.axis_index("op"), lax.axis_index("sec")
     xh, y, z = op // (Y * Z), (op // Z) % Y, op % Z
@@ -78,6 +78,9 @@
     for i in (2, 3, 4, 5):
         loads[i].start()
     pl.semaphore_wait(barrier, 6 + jnp.where(z < HUB, z, HUB))
+
+    def arrived(ref, sem):
+        pltpu.make_async_copy(ref, ref, sem).wait()
 
     def ways(step):
         cross = (sec == 1) if step == 0 else (sec == 2)
@@ -92,8 +95,8 @@
                     pltpu.make_async_remote_copy(
                         src_ref=wv.at[v, part_rows],
                         dst_ref=got.at[slot, v, part_rows],
-                        send_sem=ex_send.at[slot, half, v],
-                        recv_sem=ex_recv.at[slot, half, v],
+                        send_sem=ex_send.at[slot, v],
+                        recv_sem=ex_recv.at[slot, v],
                         device_id=(op if half == 0 else second, target),
                         device_id_type=MESH,
                     )
@@ -180,12 +183,11 @@
                 part[c][q, v] = p[k, q]
 
     for v in range(VECS):
-        for copies, edge, slot, i in ((to_next, sec > 0, 0, 0), (to_prev, sec < 3, 1, 2)):
+        for edge, slot, i in ((sec > 0, 0, 0), (sec < 3, 1, 2)):
 
             @pl.when(edge)
             def _():
-                for c in copies[2 * v : 2 * v + 2]:
-                    c.wait_recv()
+                arrived(got.at[slot, v], ex_recv.at[slot, v])
                 h, l = split(got[slot, v])
                 sh[v, i] = h
                 sl[v, i] = l
@@ -203,8 +205,8 @@
         return pltpu.make_async_remote_copy(
             src_ref=part[c].at[to],
             dst_ref=near_buf[c].at[i],
-            send_sem=near_send.at[c, i],
-            recv_sem=near_recv.at[c, i],
+            send_sem=near_send.at[c],
+            recv_sem=near_recv.at[c],
             device_id=(to * Z + z, sec),
             device_id_type=MESH,
         )
@@ -227,15 +229,14 @@
         return pltpu.make_async_remote_copy(
             src_ref=zsrc.at[c, pl.ds(j * 8, 8)],
             dst_ref=zbuf.at[slot],
-            send_sem=z_send.at[to],
-            recv_sem=z_recv.at[slot],
+            send_sem=z_sem.at[0],
+            recv_sem=z_sem.at[1],
             device_id=place(xh, y, to),
             device_id_type=MESH,
         )
 
     for c in range(PARTS):
-        for n in near[c]:
-            n.wait_recv()
+        arrived(near_buf[c], near_recv.at[c])
         total = part[c][xh * Y + y]
         for i in range(len(NEAR)):
             total = total + near_buf[c][i]
@@ -269,46 +270,33 @@
             def _():
                 far_copy(c, j).start()
 
-    for k in range(Z - 1):
-        pltpu.make_async_remote_copy(
-            src_ref=zsrc.at[0, pl.ds(0, 8)],
-            dst_ref=zbuf.at[k],
-            send_sem=z_send.at[0],
-            recv_sem=z_recv.at[k],
-            device_id=place(xh, y, (z + 1) % Z),
-            device_id_type=MESH,
-        ).wait_recv()
+    @pl.when(sec < 3)
+    def _():
+        for v in range(VECS):
+            arrived(wv.at[v], ex_send.at[0, v])
+
+    @pl.when(sec > 0)
+    def _():
+        for v in range(VECS):
+            arrived(wv.at[v], ex_send.at[1, v])
+
+    for c in range(PARTS):
+        arrived(near_buf[c], near_send.at[c])
+    arrived(zbuf, z_sem.at[0])
+
     mine, first = 0, 0
     for c in range(1, PARTS):
         mine = jnp.where(z >= ENDS[c], c, mine)
         first = jnp.where(z >= ENDS[c], ENDS[c], first)
     tile = zsrc[mine, pl.ds(pl.multiple_of((z - first) * 8, 8), 8)]
+    sub = lax.broadcasted_iota(jnp.int32, (8, 128), 0)
+    own_row = 2 * op + jnp.where(sub >= 4, 1, 0)
+    arrived(zbuf, z_sem.at[1])
     for k in range(Z - 1):
         tile = tile + zbuf[k]
-    sub = lax.broadcasted_iota(jnp.int32, (8, 128), 0)
-    own_row = 2 * op + jnp.where(sub >= 4, 1, 0)
     tile = jnp.where(own_row < rows, tile, 0.0)
     for s in range(2):
         out_ref[pl.ds(s, 4, stride=2), :] = tile[4 * s : 4 * s + 4]
-
-    @pl.when(sec < 3)
-    def _():
-        for c in to_next:
-            c.wait_send()
-
-    @pl.when(sec > 0)
-    def _():
-        for c in to_prev:
-            c.wait_send()
-
-    for c in range(PARTS):
-        for n in near[c]:
-            n.wait_send()
-        for j in range(ENDS[c + 1] - ENDS[c]):
-
-            @pl.when(ENDS[c] + j != z)
-            def _():
-                far_copy(c, j).wait_send()
 
 
 def shards(wavefunction, left_ops, right_ops, term_shift, term_count, sector_dims):
@@ -338,12 +326,11 @@
             vmem((PARTS, 4 * max(CUT), 128), F32),
             vmem((Z - 1, 8, 128), F32),
             dma((6,)),
-            dma((2, 2, VECS)),
-            dma((2, 2, VECS)),
-            dma((PARTS, n)),
-            dma((PARTS, n)),
-            dma((Z,)),
-            dma((Z - 1,)),
+            dma((2, VECS)),
+            dma((2, VECS)),
+            dma((PARTS,)),
+            dma((PARTS,)),
+            dma((2,)),
             pltpu.SemaphoreType.REGULAR((5,)),
         ],
         compiler_params=pltpu.CompilerParams(

time: 34.6 us -> 33.8 us (0.977)
  Pallas kernels: 32.4 us -> 31.7 us
    pallas_call x1, Pallas kernels: 32.4 us -> 31.7 us  [shards(): pl.pallas_call(kernel, out_shape=vmem((8, 128), F32), in_specs=[pl.BlockS...]
where the time goes in v4:
time: 33.8 us; the launch traced here: 33.6 us
  Pallas kernels  31.7 us (94%)
  between operations  1.3 us (4%)
  local copies, waits for them, and re-layouts  0.6 us (2%)
    pallas_call x1, Pallas kernels, shards(): pl.pallas_call(kernel, out_shape=vmem((8, 128), F32), in_specs=[pl.BlockS...  31.7 us

profile of v4, /device:TPU:1, one launch (start us, length us, event | category | flops | bytes accessed | tf_op | source)
XLA Modules:
  0.0 33.6 jit_solution(6844914953048325812)
XLA Ops:
  1.3 31.7 %shard_map.64 = f32[8,128]{1,0:T(8,128)S(1)} custom-call(s32[8]{0:T(128)} %shift_hbm.1, s32[1]{0:T(128)S(6)} %copy.10.count_hbm, s32[1]{0:T(128)S(6)} %copy.11.dims_hbm, f32[2,256,256]{2,1,0:T(8,128)} %bitcast.11, f32[8,256,256]{2,1,0:T(8,128)} %bitcast.9, f32[8,256,256]{2,1,0:T(8,128)} %bitcast.10), custom_call_target="tpu_custom_call" | custom-call | flops 3221225472 | bytes 4718592 | tf_op jit(solution)/shard_map/pallas_call | solution.py:305
  33.0 0.6 %copy.9 = f32[2,1,2,256]{3,2,1,0:T(2,128)} copy(f32[2,1,2,256]{3,2,1,0:T(2,128)S(1)} %bitcast.8) | data formatting | bytes 8192

commit v5 on v4

--- a/solution.py
+++ b/solution.py
@@ -30,7 +30,7 @@
 def kernel(
     shift_hbm, count_hbm, dims_hbm, w_hbm, l_hbm, r_hbm, out_ref,
     shift_ref, count_ref, dims_ref, wv, lv, rv, got, sh, sl, ls, rh, rl, gs, part, near_buf, zsrc, zbuf,
-    load_sem, ex_send, ex_recv, near_send, near_recv, z_sem, know,
+    load_sem, own_sem, ex_send, ex_recv, near_send, near_recv, z_sem, know,
 ):
     op, sec = lax.axis_index("op"), lax.axis_index("sec")
     xh, y, z = op // (Y * Z), (op // Z) % Y, op % Z
@@ -47,8 +47,15 @@
             ((dims_hbm, dims_ref), (w_hbm, wv), (l_hbm, lv), (r_hbm, rv), (shift_hbm, shift_ref), (count_hbm, count_ref))
         )
     ]
+    quarter = B // 2
+    own = [
+        pltpu.make_async_copy(w_hbm.at[v, pl.ds(h * quarter, quarter)], wv.at[v, pl.ds(h * quarter, quarter)], own_sem.at[v, h])
+        for v in range(VECS)
+        for h in range(2)
+    ]
+    for c in own:
+        c.start()
     loads[0].start()
-    loads[1].start()
 
     barrier = pltpu.get_barrier_semaphore()
     other_op = (1 - xh) * (Y * Z) + y * Z + z
@@ -70,13 +77,12 @@
                 signal(barrier, place(xh, y, (z + d) % Z))
 
     loads[0].wait()
-    loads[1].wait()
     rows = dims_ref[0]
     row = lax.broadcasted_iota(jnp.int32, (B, B), 0)
     for v in range(VECS):
+        own[2 * v].wait()
+        own[2 * v + 1].wait()
         wv[v] = jnp.where(row < rows, wv[v], 0.0)
-    for i in (2, 3, 4, 5):
-        loads[i].start()
     pl.semaphore_wait(barrier, 6 + jnp.where(z < HUB, z, HUB))
 
     def arrived(ref, sem):
@@ -114,6 +120,9 @@
     def _():
         for c in to_prev:
             c.start()
+
+    for i in (2, 3, 4, 5):
+        loads[i].start()
 
     for target in beside:
         signal(know.at[0], target)
@@ -326,6 +335,7 @@
             vmem((PARTS, 4 * max(CUT), 128), F32),
             vmem((Z - 1, 8, 128), F32),
             dma((6,)),
+            dma((VECS, 2)),
             dma((2, VECS)),
             dma((2, VECS)),
             dma((PARTS,)),

time: 33.8 us -> 33.8 us (level)
  no operation moved by 1% of the time
where the time goes in v5:
time: 33.8 us; the launch traced here: 33.6 us
  Pallas kernels  31.7 us (94%)
  between operations  1.3 us (4%)
  local copies, waits for them, and re-layouts  0.6 us (2%)
    pallas_call x1, Pallas kernels, shards(): pl.pallas_call(kernel, out_shape=vmem((8, 128), F32), in_specs=[pl.BlockS...  31.7 us

profile of v5, /device:TPU:1, one launch (start us, length us, event | category | flops | bytes accessed | tf_op | source)
XLA Modules:
  0.0 33.6 jit_solution(8466787986021755892)
XLA Ops:
  1.3 31.7 %shard_map.64 = f32[8,128]{1,0:T(8,128)S(1)} custom-call(s32[8]{0:T(128)} %shift_hbm.1, s32[1]{0:T(128)S(6)} %copy.10.count_hbm, s32[1]{0:T(128)S(6)} %copy.11.dims_hbm, f32[2,256,256]{2,1,0:T(8,128)} %bitcast.11, f32[8,256,256]{2,1,0:T(8,128)} %bitcast.9, f32[8,256,256]{2,1,0:T(8,128)} %bitcast.10), custom_call_target="tpu_custom_call" | custom-call | flops 3221225472 | bytes 4718592 | tf_op jit(solution)/shard_map/pallas_call | solution.py:314
  33.0 0.6 %copy.9 = f32[2,1,2,256]{3,2,1,0:T(2,128)} copy(f32[2,1,2,256]{3,2,1,0:T(2,128)S(1)} %bitcast.8) | data formatting | bytes 8192

commit v6 on v4

--- a/solution.py
+++ b/solution.py
@@ -212,7 +212,8 @@
         )
 
     near = [[near_copy(c, a, b) for a, b in NEAR] for c in range(PARTS)]
-    for c in range(PARTS):
+
+    def make(c):
         if c > 0:
             for v in range(VECS):
                 left(c, v)
@@ -235,7 +236,7 @@
             device_id_type=MESH,
         )
 
-    for c in range(PARTS):
+    def onward(c):
         arrived(near_buf[c], near_recv.at[c])
         total = part[c][xh * Y + y]
         for i in range(len(NEAR)):
@@ -269,6 +270,13 @@
             @pl.when(ENDS[c] + j != z)
             def _():
                 far_copy(c, j).start()
+
+    make(0)
+    make(1)
+    onward(0)
+    make(2)
+    onward(1)
+    onward(2)
 
     @pl.when(sec < 3)
     def _():

time: 33.8 us -> 33.7 us (level)
  no operation moved by 1% of the time
where the time goes in v6:
time: 33.7 us; the launch traced here: 33.3 us
  Pallas kernels  31.4 us (93%)
  between operations  1.3 us (4%)
  local copies, waits for them, and re-layouts  0.6 us (2%)
    pallas_call x1, Pallas kernels, shards(): pl.pallas_call(kernel, out_shape=vmem((8, 128), F32), in_specs=[pl.BlockS...  31.4 us

profile of v6, /device:TPU:1, one launch (start us, length us, event | category | flops | bytes accessed | tf_op | source)
XLA Modules:
  0.0 33.3 jit_solution(3175111887570693078)
XLA Ops:
  1.3 31.4 %shard_map.64 = f32[8,128]{1,0:T(8,128)S(1)} custom-call(s32[8]{0:T(128)} %shift_hbm.1, s32[1]{0:T(128)S(6)} %copy.10.count_hbm, s32[1]{0:T(128)S(6)} %copy.11.dims_hbm, f32[2,256,256]{2,1,0:T(8,128)} %bitcast.11, f32[8,256,256]{2,1,0:T(8,128)} %bitcast.9, f32[8,256,256]{2,1,0:T(8,128)} %bitcast.10), custom_call_target="tpu_custom_call" | custom-call | flops 3221225472 | bytes 4718592 | tf_op jit(solution)/shard_map/pallas_call | solution.py:313
  32.8 0.6 %copy.9 = f32[2,1,2,256]{3,2,1,0:T(2,128)} copy(f32[2,1,2,256]{3,2,1,0:T(2,128)S(1)} %bitcast.8) | data formatting | bytes 8192
